TPU v7x, 32 devices: a whole 2x2x4 slice. The times are simulated.
32 devices in a mesh: tok: 4 (over z), tp: 4 (over y, x), grp: 2 (over core).
Axes of the slice: x: 2, y: 2, z: 4, core: 2. Of those that a mesh axis runs over, the one named last changes fastest.
Arguments:
- hidden: bfloat16 [1024, 6144], P(('tok', 'grp'), 'tp'), may hold values from -6 to 6
- gain: bfloat16 [6144], P('tp'), may hold values from 0.5 to 1.5
- expert_ids: int32 [1024, 2], P(('tok', 'grp')), may hold values from 0 to 3, all different within a row; in each aligned block of 128 rows (0 to 127, 128 to 255, ...) at most 80 rows name the same one
- gate_weights: float32 [1024, 2], P(('tok', 'grp')), may hold values from 0.1 to 0.9
- segment_ids: int32 [1024], P(('tok', 'grp')), may hold values from 0 to 7, never falling along the last dimension, each value on 1 to 384 neighbouring positions
- upstream: bfloat16 [1024, 6144], P(('tok', 'grp'), 'tp'), may hold values from -6 to 6
- w_gate: bfloat16 [4, 6144, 8192], P('tok', None, ('tp', 'grp')), may hold values from -0.078125 to 0.078125
- w_up: bfloat16 [4, 6144, 8192], P('tok', None, ('tp', 'grp')), may hold values from -0.078125 to 0.078125
- w_down: bfloat16 [4, 8192, 6144], P('tok', ('tp', 'grp')), may hold values from -0.0625 to 0.0625
Outputs:
- mixed: bfloat16 [1024, 6144], P(('tok', 'grp'), 'tp')
- importance: float32 [4, 8192], P('tok', ('tp', 'grp'))
Inputs may be any that keep to these rules, and one draw needn't show every extreme that they name: `expert_ids`: each token names 2 different experts. Within the tokens of one token shard (aligned blocks of 128 rows) no expert is named by more than 80 tokens, and in some block one expert is named by exactly 80. `segment_ids`: never falling along the tokens; every document holds between 1 and 384 tokens.
All inputs are finite; a program needn't handle non-finite values.
Results may differ from a plain program's by a relative error of at most 0.0095.
Values may be sent and summed in bfloat16 or wider, within the bound.
A program may use at most 128 MiB of HBM per device.

v0:
```python
import jax
import jax.numpy as jnp
from jax import lax
from jax.sharding import PartitionSpec as P


def expert_pass(rows_in, cot_in, gate_mat, up_mat, down_mat):
    gate_pre = jnp.dot(rows_in, gate_mat, preferred_element_type=jnp.float32)
    up_proj = jnp.dot(rows_in, up_mat, preferred_element_type=jnp.float32)
    sigmoid_gate = jax.nn.sigmoid(gate_pre)
    activated = gate_pre * sigmoid_gate
    hidden_act = (activated * up_proj).astype(jnp.bfloat16)
    grad_act = lax.dot_general(
        cot_in, down_mat, (((1,), (1,)), ((), ())), preferred_element_type=jnp.float32
    )
    grad_gate = (
        grad_act * up_proj * sigmoid_gate * (1.0 + gate_pre * (1.0 - sigmoid_gate))
    ).astype(jnp.bfloat16)
    grad_up = (grad_act * activated).astype(jnp.bfloat16)
    grad_wgate = lax.dot_general(
        rows_in, grad_gate, (((0,), (0,)), ((), ())), preferred_element_type=jnp.float32
    )
    grad_wup = lax.dot_general(
        rows_in, grad_up, (((0,), (0,)), ((), ())), preferred_element_type=jnp.float32
    )
    grad_wdown = lax.dot_general(
        hidden_act, cot_in, (((0,), (0,)), ((), ())), preferred_element_type=jnp.float32
    )
    scores = jnp.sum(jnp.abs(grad_wgate * gate_mat.astype(jnp.float32)), axis=0)
    scores = scores + jnp.sum(jnp.abs(grad_wup * up_mat.astype(jnp.float32)), axis=0)
    scores = scores + jnp.sum(jnp.abs(grad_wdown * down_mat.astype(jnp.float32)), axis=1)
    return (hidden_act, scores)


def on_device(hidden, gain, expert_ids, gate_weights, segment_ids, upstream, w_gate, w_up, w_down):
    rows_here = hidden.shape[0]
    top_count = expert_ids.shape[1]
    experts = lax.axis_size("tok")
    groups = lax.axis_size("grp")
    capacity = 5 * rows_here // (2 * experts)
    width = w_gate.shape[1]
    documents = jnp.arange(experts * groups, dtype=jnp.int32)
    doc_onehot = (segment_ids[:, None] == documents[None, :]).astype(jnp.float32)
    doc_len = lax.psum(jnp.sum(doc_onehot, axis=0), ("tok", "grp"))
    tok_len = jnp.sum(doc_onehot * doc_len[None, :], axis=1)
    tok_weight = rows_here / tok_len
    onehot = (
        expert_ids.reshape(-1)[:, None] == jnp.arange(experts, dtype=jnp.int32)[None, :]
    ).astype(jnp.int32)
    before = jnp.cumsum(onehot, axis=0) - onehot
    slot_ids = jnp.sum(before * onehot, axis=1).reshape(rows_here, top_count)
    targets = expert_ids * capacity + slot_ids
    all_slots = jnp.arange(experts * capacity, dtype=jnp.int32)
    matches = all_slots[:, None, None] == targets[None, :, :]
    placing = jnp.any(matches, axis=2).astype(jnp.bfloat16)
    scaled = gate_weights * tok_weight[:, None]
    slot_scale = jnp.sum(jnp.where(matches, scaled[None, :, :], 0.0), axis=(1, 2))
    combining = jnp.sum(jnp.where(matches, gate_weights[None, :, :], 0.0), axis=2)
    wide_hidden = hidden.astype(jnp.float32)
    squares = lax.psum(jnp.sum(wide_hidden * wide_hidden, axis=1), "tp")
    scaling = lax.rsqrt(squares / width + 1e-05)
    normed = (wide_hidden * scaling[:, None] * gain.astype(jnp.float32)[None, :]).astype(
        jnp.bfloat16
    )
    block_rows = jnp.dot(placing, normed, preferred_element_type=jnp.float32).astype(jnp.bfloat16)
    block_cot = jnp.dot(placing, upstream, preferred_element_type=jnp.float32) * slot_scale[:, None]
    block_rows = block_rows.reshape(experts, capacity, -1)
    block_cot = block_cot.astype(jnp.bfloat16).reshape(experts, capacity, -1)
    came_rows, came_cot = (
        lax.all_to_all(block_rows, "tok", split_axis=0, concat_axis=0, tiled=True),
        lax.all_to_all(block_cot, "tok", split_axis=0, concat_axis=0, tiled=True),
    )
    part_rows, part_cot = (
        lax.all_gather(came_rows, "tp", axis=2, tiled=True),
        lax.all_gather(came_cot, "tp", axis=2, tiled=True),
    )
    pooled_rows, pooled_cot = (
        lax.all_gather(part_rows, "grp", axis=0, tiled=True),
        lax.all_gather(part_cot, "grp", axis=0, tiled=True),
    )
    rows_in = pooled_rows.reshape(-1, width)
    cot_in = pooled_cot.reshape(-1, width)
    gate_mat = w_gate[0]
    up_mat = w_up[0]
    down_mat = w_down[0]
    hidden_act, scores = expert_pass(rows_in, cot_in, gate_mat, up_mat, down_mat)
    importance = scores / (rows_here * experts * groups)
    partial_value = lax.psum_scatter(
        lax.dot_general(
            down_mat, hidden_act, (((0,), (1,)), ((), ())), preferred_element_type=jnp.float32
        ).astype(jnp.bfloat16),
        "tp",
        scatter_dimension=0,
        tiled=True,
    )
    summed = lax.psum_scatter(partial_value, "grp", scatter_dimension=1, tiled=True).astype(
        jnp.float32
    )
    slice_width = summed.shape[0]
    outgoing = summed.astype(jnp.bfloat16).reshape(slice_width, experts, capacity)
    returned = lax.all_to_all(outgoing, "tok", split_axis=1, concat_axis=1, tiled=True)
    returned = returned.reshape(slice_width, experts * capacity).astype(jnp.float32)
    combined = lax.dot_general(
        combining,
        returned,
        (((0,), (1,)), ((), ())),
        precision=lax.Precision.HIGHEST,
        preferred_element_type=jnp.float32,
    )
    mixed = (hidden.astype(jnp.float32) + combined).astype(jnp.bfloat16)
    return (mixed, importance[None, :])


def solution(mesh):
    placed = (
        P(("tok", "grp"), "tp"),
        P("tp"),
        P(("tok", "grp"), None),
        P(("tok", "grp"), None),
        P(("tok", "grp")),
        P(("tok", "grp"), "tp"),
        P("tok", None, ("tp", "grp")),
        P("tok", None, ("tp", "grp")),
        P("tok", ("tp", "grp"), None),
    )
    return jax.shard_map(
        on_device,
        mesh=mesh,
        in_specs=placed,
        out_specs=(P(("tok", "grp"), "tp"), P("tok", ("tp", "grp"))),
        check_vma=False,
    )
```

profile of v0, /device:TPU:0, one launch (start us, length us, event | category | flops | bytes accessed | tf_op | source)
XLA Modules:
  0.0 371.6 jit_solution(5558731557900646334)
XLA Ops:
  7.2 0.0 copy-start
  7.2 0.0 copy-start.5
  7.2 0.0 copy-start.3
  7.2 0.0 all-gather.5.cloned.1.call-start
  7.2 0.8 copy.39
  8.1 0.1 eq.56
  8.2 0.1 eq.52
  8.4 1.2 fusion.18
  9.5 11.4 %psum.14 = f32[128]{0:T(128)S(1)} all-reduce(f32[128]{0:T(128)S(1)} %fusion.18), channel_id=1, replica_groups=mesh['tok'=4,'tp'=4,'grp'=2] {'tp'}, use_global_device_ids=true, to_apply=%region_6.7 | all-reduce | flops 128 | bytes 1024 | tf_op jit(solution)/shard_map/psum | solution.py:60
  20.9 0.7 convert_element_type.60
  21.6 1.2 reduce-window.6
  22.8 0.1 slice.8
  22.9 0.1 copy.41
  23.0 0.1 copy.42
  23.1 0.1 add_bitcast_fusion
  23.2 0.1 reshape.79
  23.3 0.1 copy.43
  23.4 0.7 multiply_add_fusion
  24.2 1.5 convolution_convert_fusion
  25.7 27.1 %all_to_all.15 = bf16[4,80,1536]{2,1,0:T(8,128)(2,1)} all-to-all(bf16[4,80,1536]{2,1,0:T(8,128)(2,1)S(1)} %bitcast.62), channel_id=1, replica_groups=mesh['tok'=4,'tp'=4,'grp'=2] {'tok'}, dimensions={0} | all-to-all | bytes 1966080 | tf_op jit(solution)/shard_map/all_to_all | solution.py:70
  52.7 0.0 all-gather.5.cloned.1.call-update
  52.8 0.0 all-gather.9.cloned.1.call-start
  52.8 0.0 copy-done.5
  52.8 0.1 convert_reduce_fusion
  52.9 13.6 %psum.15 = f32[8]{0:T(128)S(1)} all-reduce(f32[8]{0:T(128)S(1)} %convert_reduce_fusion), channel_id=1, replica_groups=mesh['tok'=4,'tp'=4,'grp'=2] {'tok','grp'}, use_global_device_ids=true, to_apply=%region_10.11 | all-reduce | flops 8 | bytes 64 | tf_op jit(solution)/shard_map/psum | solution.py:44
  66.5 0.1 select_reduce_fusion.2
  66.6 0.0 copy-done.3
  66.6 0.1 select_reduce_fusion
  66.8 0.0 copy-done
  66.8 0.4 fusion.14
  67.2 27.8 %all_to_all.16 = bf16[4,80,1536]{2,1,0:T(8,128)(2,1)} all-to-all(bf16[4,80,1536]{2,1,0:T(8,128)(2,1)S(1)} %bitcast.63), channel_id=1, replica_groups=mesh['tok'=4,'tp'=4,'grp'=2] {'tok'}, dimensions={0} | all-to-all | bytes 1966080 | tf_op jit(solution)/shard_map/all_to_all | solution.py:71
  95.0 0.0 all-gather.9.cloned.1.call-update
  95.0 0.0 all-gather.7.cloned.1.call-start
  95.1 5.7 %all-gather.5.cloned.1.call-done = bf16[4,80,6144]{2,1,0:T(8,128)(2,1)} async-done(((bf16[4,80,1536]{2,1,0:T(8,128)(2,1)}), bf16[4,80,6144]{2,1,0:T(8,128)(2,1)}) %all-gather.5.cloned.1.call-update) | async-done | bytes 3932176 | tf_op jit(solution)/shard_map/all_gather | solution.py:74
  100.8 0.0 all-gather.7.cloned.1.call-update
  100.8 0.0 all-gather.11.cloned.1.call-start
  100.9 52.3 %all-gather.9.cloned.1.call-done = bf16[4,80,6144]{2,1,0:T(8,128)(2,1)} async-done(((bf16[4,80,1536]{2,1,0:T(8,128)(2,1)}), bf16[4,80,6144]{2,1,0:T(8,128)(2,1)}) %all-gather.9.cloned.1.call-update) | async-done | bytes 3932176 | tf_op jit(solution)/shard_map/all_gather | solution.py:75
  153.2 0.0 all-gather.11.cloned.1.call-update
  153.2 0.0 reduce-scatter.3.cloned.1.call-start
  153.3 20.6 %all-gather.7.cloned.1.call-done = bf16[8,80,6144]{2,1,0:T(8,128)(2,1)} async-done(((bf16[4,80,6144]{2,1,0:T(8,128)(2,1)}), bf16[8,80,6144]{2,1,0:T(8,128)(2,1)}) %all-gather.7.cloned.1.call-update) | async-done | bytes 7864336 | tf_op jit(solution)/shard_map/all_gather | solution.py:78
  173.9 14.7 %fusion.6 = f32[640,1024]{1,0:T(8,128)} fusion(bf16[640,6144]{1,0:T(8,128)(2,1)} %bitcast.69, bf16[1,6144,1024]{2,1,0:T(8,128)(2,1)} %param.15), kind=kOutput, calls=%fused_computation.9 | convolution fusion | flops 8053063680 | bytes 23068672 | tf_op jit(solution)/shard_map/dot_general | solution.py:8
  188.6 0.0 copy-done.4
  188.6 14.4 %multiply_convert_fusion.2 = (bf16[640,1024]{1,0:T(8,128)(2,1)S(1)}, f32[640,1024]{1,0:T(8,128)}) fusion(f32[640,1024]{1,0:T(8,128)} %fusion.6, bf16[640,6144]{1,0:T(8,128)(2,1)S(1)} %bitcast.72, bf16[1,6144,1024]{2,1,0:T(8,128)(2,1)} %param.16), kind=kOutput, calls=%fused_computation.18 | convolution fusion | flops 8056995840 | bytes 27000832 | tf_op jit(solution)/shard_map/dot_general | solution.py:9
  203.1 0.0 slice-done
  203.1 0.0 slice-done.1
  203.1 0.0 slice-done.2
  203.1 10.3 %fusion.11 = bf16[6144,640]{0,1:T(8,128)(2,1)} fusion(bf16[640,1024]{1,0:T(8,128)(2,1)S(1)} %get-tuple-element.4, bf16[1,1024,6144]{2,1,0:T(8,128)(2,1)S(1)} %bitcast.68), kind=kOutput, calls=%fused_computation.12 | convolution fusion | flops 8056995840 | bytes 21757952 | tf_op jit(solution)/shard_map/dot_general | solution.py:89
  213.4 0.0 reduce-scatter.3.cloned.1.call-update
  213.4 0.2 reduce-scatter.5.cloned.1.call-start
  213.7 0.0 all-gather.11.cloned.1.call-done
  213.7 14.7 %fusion = f32[640,1024]{1,0:T(8,128)} fusion(bf16[640,6144]{1,0:T(8,128)(2,1)} %bitcast.73, bf16[1,1024,6144]{2,1,0:T(8,128)(2,1)} %param.17), kind=kOutput, calls=%fused_computation.3 | convolution fusion | flops 8053063680 | bytes 23068672 | tf_op jit(solution)/shard_map/dot_general | solution.py:13
  228.4 69.7 %reduce-scatter.3.cloned.1.call-done = bf16[1536,640]{0,1:T(8,128)(2,1)} async-done(((bf16[6144,640]{0,1:T(8,128)(2,1)}), bf16[1536,640]{0,1:T(8,128)(2,1)}) %reduce-scatter.3.cloned.1.call-update) | async-done | bytes 1966096 | tf_op jit(solution)/shard_map/reduce_scatter | solution.py:88
  298.1 0.0 reduce-scatter.5.cloned.1.call-update
  298.2 0.0 copy-start.6
  298.2 0.0 copy-start.7
  298.2 19.9 %abs_reduce_fusion.1 = f32[1024]{0:T(1024)S(1)} fusion(bf16[1,6144,1024]{2,1,0:T(8,128)(2,1)} %param.16, bf16[640,6144]{1,0:T(8,128)(2,1)} %bitcast.70, f32[640,1024]{1,0:T(8,128)} %fusion, f32[640,1024]{1,0:T(8,128)} %fusion.6), kind=kOutput, calls=%fused_computation.1 | convolution fusion | flops 8082160640 | bytes 25694208 | tf_op jit(solution)/shard_map/dot_general | solution.py:23
  318.1 16.1 %abs_reduce_fusion.2 = f32[1024]{0:T(1024)S(1)} fusion(bf16[1,6144,1024]{2,1,0:T(8,128)(2,1)} %param.15, bf16[640,6144]{1,0:T(8,128)(2,1)} %bitcast.71, f32[640,1024]{1,0:T(8,128)S(1)} %copy-done.6, f32[640,1024]{1,0:T(8,128)S(1)} %copy-done.8, f32[640,1024]{1,0:T(8,128)S(1)} %copy-done.7), kind=kOutput, calls=%fused_computation.2 | convolution fusion | flops 8084782080 | bytes 28315648 | tf_op jit(solution)/shard_map/dot_general | solution.py:20
  334.2 0.0 reduce-scatter.5.cloned.1.call-done
  334.3 4.6 %all-to-all-start.1 = ((bf16[1536,4,80]{0,2,1:T(8,128)(2,1)}), bf16[1536,4,80]{0,2,1:T(8,128)(2,1)S(1)}, u32[]{:S(2)}, u32[]{:S(2)}) async-start(bf16[1536,4,80]{0,2,1:T(8,128)(2,1)} %bitcast.64), calls=%async_computation.3 | async-start | bytes 1966080 | tf_op jit(solution)/shard_map/all_to_all | solution.py:101
  338.9 17.0 %abs_reduce_fusion = f32[1024]{0:T(1024)S(1)} fusion(bf16[640,1024]{1,0:T(8,128)(2,1)S(1)} %get-tuple-element.4, bf16[640,6144]{1,0:T(8,128)(2,1)} %bitcast.74, bf16[1,1024,6144]{2,1,0:T(8,128)(2,1)} %param.17), kind=kOutput, calls=%fused_computation | convolution fusion | flops 8078228480 | bytes 21762048 | tf_op jit(solution)/shard_map/dot_general | solution.py:26
  355.8 0.6 add_multiply_fusion
  356.4 6.7 %all-to-all-done.1 = bf16[1536,4,80]{0,2,1:T(8,128)(2,1)S(1)} async-done(((bf16[1536,4,80]{0,2,1:T(8,128)(2,1)}), bf16[1536,4,80]{0,2,1:T(8,128)(2,1)S(1)}, u32[]{:S(2)}, u32[]{:S(2)}) %all-to-all-start.1) | async-done | bytes 983072 | tf_op jit(solution)/shard_map/all_to_all | solution.py:101
  363.2 1.6 fusion.16
  364.8 0.0 copy-done.1
  (20 shorter events, 0.1 us)
Async XLA Ops:
  7.2 59.6 %copy-start = (bf16[128,1536]{1,0:T(8,128)(2,1)S(1)}, bf16[128,1536]{1,0:T(8,128)(2,1)}, u32[]{:S(2)}) copy-start(bf16[128,1536]{1,0:T(8,128)(2,1)} %param.14) | copy-start | bytes 1179652
  7.2 45.6 %copy-start.5 = (s32[128]{0:T(128)S(1)}, s32[128]{0:T(128)}, u32[]{:S(2)}) copy-start(s32[128]{0:T(128)} %param.13) | copy-start | bytes 1540
  7.2 59.4 %copy-start.3 = (f32[128,2]{0,1:T(2,128)S(1)}, f32[128,2]{0,1:T(2,128)}, u32[]{:S(2)}) copy-start(f32[128,2]{0,1:T(2,128)} %param.12) | copy-start | bytes 3076
  7.2 93.6 %all-gather.5.cloned.1.call-start = ((), (), s32[]{:S(2)}) async-start(), calls=%async_computation.5 | async-start | bytes 4915200 | tf_op jit(solution)/shard_map/all_gather | solution.py:74
  52.8 100.5 %all-gather.9.cloned.1.call-start = ((), (), s32[]{:S(2)}) async-start(), calls=%async_computation.9 | async-start | bytes 4915200 | tf_op jit(solution)/shard_map/all_gather | solution.py:75
  95.0 78.9 %all-gather.7.cloned.1.call-start = ((), (), s32[]{:S(2)}) async-start(), calls=%async_computation.6 | async-start | bytes 11796480 | tf_op jit(solution)/shard_map/all_gather | solution.py:78
  100.8 112.8 %all-gather.11.cloned.1.call-start = ((), (), s32[]{:S(2)}) async-start(), calls=%async_computation.10 | async-start | bytes 11796480 | tf_op jit(solution)/shard_map/all_gather | solution.py:79
  153.2 144.9 %reduce-scatter.3.cloned.1.call-start = ((), (), s32[]{:S(2)}) async-start(), calls=%async_computation.7 | async-start | bytes 9830400 | tf_op jit(solution)/shard_map/reduce_scatter | solution.py:88
  173.9 14.7 %copy-start.4 = (bf16[8,80,6144]{2,1,0:T(8,128)(2,1)S(1)}, bf16[8,80,6144]{2,1,0:T(8,128)(2,1)}, u32[]{:S(2)}) copy-start(bf16[8,80,6144]{2,1,0:T(8,128)(2,1)} %all-gather.7.cloned.1.call-done) | copy-start | bytes 23592964
  173.9 29.2 %slice-start = ((s8[12582912]{0:T(1024)(128)(4,1)}), s8[4194304]{0:T(1024)(128)(4,1)S(1)}, s32[]{:S(2)}) async-start(s8[12582912]{0:T(1024)(128)(4,1)} %bitcast.67), calls=%async_computation.11 | async-start | bytes 8388608
  173.9 29.2 %slice-start.1 = ((s8[12582912]{0:T(1024)(128)(4,1)}), s8[4194304]{0:T(1024)(128)(4,1)S(1)}, s32[]{:S(2)}) async-start(s8[12582912]{0:T(1024)(128)(4,1)} %bitcast.67), calls=%async_computation.12 | async-start | bytes 8388608
  188.6 14.4 %slice-start.2 = ((s8[12582912]{0:T(1024)(128)(4,1)}), s8[4194304]{0:T(1024)(128)(4,1)S(1)}, s32[]{:S(2)}) async-start(s8[12582912]{0:T(1024)(128)(4,1)} %bitcast.67), calls=%async_computation.13 | async-start | bytes 8388608
  213.4 120.8 %reduce-scatter.5.cloned.1.call-start = ((), (), s32[]{:S(2)}) async-start(), calls=%async_computation.8 | async-start | bytes 2949120 | tf_op jit(solution)/shard_map/reduce_scatter | solution.py:96
  298.2 19.9 %copy-start.6 = (f32[640,1024]{1,0:T(8,128)S(1)}, f32[640,1024]{1,0:T(8,128)}, u32[]{:S(2)}) copy-start(f32[640,1024]{1,0:T(8,128)} %fusion.6) | copy-start | bytes 7864324
  298.2 19.9 %copy-start.7 = (f32[640,1024]{1,0:T(8,128)S(1)}, f32[640,1024]{1,0:T(8,128)}, u32[]{:S(2)}) copy-start(f32[640,1024]{1,0:T(8,128)} %get-tuple-element.5) | copy-start | bytes 7864324
  298.2 19.9 %copy-start.8 = (f32[640,1024]{1,0:T(8,128)S(1)}, f32[640,1024]{1,0:T(8,128)}, u32[]{:S(2)}) copy-start(f32[640,1024]{1,0:T(8,128)} %fusion) | copy-start | bytes 7864324
  334.3 28.9 %all-to-all-start.1 = ((bf16[1536,4,80]{0,2,1:T(8,128)(2,1)}), bf16[1536,4,80]{0,2,1:T(8,128)(2,1)S(1)}, u32[]{:S(2)}, u32[]{:S(2)}) async-start(bf16[1536,4,80]{0,2,1:T(8,128)(2,1)} %bitcast.64), calls=%async_computation.3 | async-start | bytes 1966080 | tf_op jit(solution)/shard_map/all_to_all | solution.py:101
  338.9 24.3 %copy-start.2 = (bf16[128,1536]{1,0:T(8,128)(2,1)S(1)}, bf16[128,1536]{1,0:T(8,128)(2,1)}, u32[]{:S(2)}) copy-start(bf16[128,1536]{1,0:T(8,128)(2,1)} %param.9) | copy-start | bytes 1179652
  338.9 25.9 %copy-start.1 = (bf16[128,1536]{1,0:T(8,128)(2,1)S(1)}, bf16[128,1536]{1,0:T(8,128)(2,1)}, u32[]{:S(2)}) copy-start(bf16[128,1536]{1,0:T(8,128)(2,1)} %param.14) | copy-start | bytes 1179652
Sparse Core Ops, SparseCore 0:
  52.9 47.8 all-gather.4
  102.7 50.5 all-gather.8
  154.8 19.0 all-gather.6
  175.3 20.2 all-gather.10
  213.5 84.5 reduce-scatter.2
  300.2 9.4 reduce-scatter.4
where the time goes:
time: 372 us
  waiting for transfers between devices  155 us (42%)
  matrix products  111 us (30%)
  blocking collectives  79.8 us (21%)
  between operations  14.3 us (4%)
  starting transfers between devices  5.04 us (1%)
  other arithmetic  4.92 us (1%)
    reduce_scatter x1, waiting for transfers between devices, on_device(): lax.psum_scatter(lax.dot_general(down_mat, hidden_act, (((0,), (1,)), (()...  69.7 us
    all_gather x1, waiting for transfers between devices, on_device(): lax.all_gather(came_cot, 'tp', axis=2, tiled=True)  52.3 us
    all_to_all x1, blocking collectives, on_device(): lax.all_to_all(block_cot, 'tok', split_axis=0, concat_axis=0, tiled=True)  27.8 us
    all_to_all x1, blocking collectives, on_device(): lax.all_to_all(block_rows, 'tok', split_axis=0, concat_axis=0, tiled=True)  27.1 us
    all_gather x1, waiting for transfers between devices, on_device(): lax.all_gather(part_rows, 'grp', axis=0, tiled=True)  20.6 us
    dot_general x1, matrix products, expert_pass(): lax.dot_general(rows_in, grad_up, (((0,), (0,)), ((), ())), preferred_ele...  19.9 us
    dot_general x1, matrix products, expert_pass(): lax.dot_general(hidden_act, cot_in, (((0,), (0,)), ((), ())), preferred_e...  17 us
    dot_general x1, matrix products, expert_pass(): lax.dot_general(rows_in, grad_gate, (((0,), (0,)), ((), ())), preferred_e...  16.1 us
  transfers between devices with their start and end apart: 7, of which 5 were waited for; matrix products, arithmetic and copies ran while one was open for 29% of the time, Pallas kernels for 0%

commit v1 on v0

v1 whole, which is shorter than its diff:
```python
import functools
import math

import jax
import jax.numpy as jnp
from jax import lax
from jax.experimental import pallas as pl
from jax.experimental.pallas import tpu as pltpu
from jax.sharding import PartitionSpec as P

MESH = pl.DeviceIdType.MESH
F32 = jnp.float32
BF16 = jnp.bfloat16


def snake(i, n):
    side = math.isqrt(n)
    if side * side != n:
        return i
    r = i // side
    q = i % side
    return r * side + q + (r % 2) * (side - 1 - 2 * q)


def tile_of(n, most):
    return most if n % most == 0 else n


def expert_kernel(
    E, T, G, C, W, H, NC, KB,
    blk_rows, blk_cot, wg, wu, wd,
    back, imp_gu, imp_dn,
    X, accg, accu, ga, act, act_t, dgu, wdv, part, part_in, sum_in, wbuf, xt,
    a2a_s, a2a_r, ring_s, ring_r, pair_s, pair_r, part_s, part_r, sum_s, sum_r, back_s, back_r, wsem, wdsem,
):
    s = lax.axis_index("tok")
    tp = lax.axis_index("tp")
    g = lax.axis_index("grp")
    p = snake(tp, T)
    right = snake((p + 1) % T, T)
    left = snake((p + T - 1) % T, T)
    other = 1 - g
    E2 = E // 2
    R2 = E2 * C
    HR = G * R2
    CR = R2 // NC
    D = T * W
    NK = W // KB
    blks = (blk_rows, blk_cot)

    def tokdev(k):
        return {"tok": (s + k) % E}

    def ringdev(d):
        return {"tp": right if d == 0 else left}

    pairdev = {"grp": other}

    barrier = pltpu.get_barrier_semaphore()
    for k in range(1, E):
        pl.semaphore_signal(barrier, inc=1, device_id=tokdev(k), device_id_type=MESH)
    for d in range(2):
        pl.semaphore_signal(barrier, inc=1, device_id=ringdev(d), device_id_type=MESH)
    pl.semaphore_signal(barrier, inc=1, device_id=pairdev, device_id_type=MESH)

    def wd_copy():
        return pltpu.make_async_copy(wd.at[0], wdv, wdsem)

    def fwd_copies(i, slot):
        h = i // (2 * NK)
        d = (i // NK) % 2
        k = i % NK
        off = d * h + (1 - d) * (T - h)
        t = snake((p + off) % T, T)
        start = pl.multiple_of(t * W + k * KB, KB)
        return [
            pltpu.make_async_copy(w.at[0, pl.ds(start, KB), :], wbuf.at[slot, m], wsem.at[slot, m])
            for m, w in enumerate((wg, wu))
        ]

    def grad_copies(j, slot):
        start = pl.multiple_of(j * KB, KB)
        return [
            pltpu.make_async_copy(w.at[0, pl.ds(start, KB), :], wbuf.at[slot, m], wsem.at[slot, m])
            for m, w in enumerate((wg, wu))
        ]

    for c in fwd_copies(0, 0):
        c.start()
    wd_copy().start()

    def group_rows(half, grp, c, n):
        return pl.ds(pl.multiple_of(half * HR + grp * R2 + c * n, 16), n)

    def a2a_copy(a, k):
        return pltpu.make_async_remote_copy(
            src_ref=blks[a].at[(s + k) % E],
            dst_ref=X.at[a, tp, group_rows(k % 2, g, k // 2, C), :],
            send_sem=a2a_s.at[a, k], recv_sem=a2a_r.at[a, k],
            device_id=tokdev(k), device_id_type=MESH,
        )

    def own_copy(a):
        return pltpu.make_async_copy(
            blks[a].at[s], X.at[a, tp, group_rows(0, g, 0, C), :], a2a_r.at[a, 0]
        )

    def slice_at(h, d):
        return snake((p + (h if d else T - h)) % T, T)

    def ring_copy(a, h, d, c, received=False):
        view = X.at[a, slice_at(h + 1 if received else h, d), group_rows(d, g, c, CR), :]
        return pltpu.make_async_remote_copy(
            src_ref=view, dst_ref=view,
            send_sem=ring_s.at[a, h, d, c], recv_sem=ring_r.at[a, h, d, c],
            device_id=ringdev(d), device_id_type=MESH,
        )

    def pair_copy(a, h, d, c, received=False):
        view = X.at[a, slice_at(h, d), group_rows(d, other if received else g, c, CR), :]
        return pltpu.make_async_remote_copy(
            src_ref=view, dst_ref=view,
            send_sem=pair_s.at[a, h, d, c], recv_sem=pair_r.at[a, h, d, c],
            device_id=pairdev, device_id_type=MESH,
        )

    pl.semaphore_wait(barrier, E + 2)
    for a in range(2):
        own_copy(a).start()
        for k in range(1, E):
            a2a_copy(a, k).start()

    def arrive(a, h):
        for c in range(NC):
            for d in range(2):
                if h == 0:
                    per = E2 // NC
                    for q in range(c * per, (c + 1) * per):
                        k = 2 * q + d
                        if k == 0:
                            own_copy(a).wait()
                        else:
                            a2a_copy(a, k).wait_recv()
                else:
                    ring_copy(a, h - 1, d, c, True).wait_recv()
                if h < T - 1:
                    ring_copy(a, h, d, c).start()
                pair_copy(a, h, d, c).start()

    def pair_arrive(a, h):
        for c in range(NC):
            for d in range(2):
                pair_copy(a, h, d, c, True).wait_recv()

    def rows_of(d):
        return pl.ds(pl.multiple_of(d * HR, 16), HR)

    def lanes(start, n, unit=128):
        return pl.ds(pl.multiple_of(start, unit), n)

    HN = tile_of(H, 256)
    WN = tile_of(W, 256)

    def zero(ref):
        def body(i, _):
            ref[pl.ds(pl.multiple_of(i * 16, 16), 16), :] = jnp.zeros((16, ref.shape[1]), F32)
            return 0
        lax.fori_loop(0, ref.shape[0] // 16, body, 0)

    def forward(h):
        pair_arrive(0, h)

        def body(i, _):
            slot = i % 2

            @pl.when(i + 1 < T * 2 * NK)
            def _():
                for c in fwd_copies(i + 1, 1 - slot):
                    c.start()

            for c in fwd_copies(i, slot):
                c.wait()
            d = (i // NK) % 2
            k = i % NK
            off = d * h + (1 - d) * (T - h)
            t = snake((p + off) % T, T)
            x = X[0, t, rows_of(d), lanes(k * KB, KB)]
            for m, acc in enumerate((accg, accu)):
                for n in range(H // HN):
                    cols = slice(n * HN, (n + 1) * HN)
                    acc[rows_of(d), cols] += jnp.dot(
                        x, wbuf[slot, m, :, cols], preferred_element_type=F32
                    )
            return 0

        lax.fori_loop(h * 2 * NK, (h + 1) * 2 * NK, body, 0)

    def activate():
        def body(i, _):
            rows = pl.ds(pl.multiple_of(i * 16, 16), 16)
            gate = accg[rows, :]
            up = accu[rows, :]
            sig = jax.nn.sigmoid(gate)
            silu = gate * sig
            act[rows, :] = (silu * up).astype(BF16)
            accg[rows, :] = up * sig * (1.0 + gate * (1.0 - sig))
            accu[rows, :] = silu
            return 0

        lax.fori_loop(0, 2 * HR // 16, body, 0)
        for n in range(H // 128):
            act_t[n * 128:(n + 1) * 128, :] = act[:, n * 128:(n + 1) * 128].T

    def gradients():
        def body(i, _):
            rows = pl.ds(pl.multiple_of(i * 16, 16), 16)
            grad = ga[rows, :]
            dgu[rows, 0:H] = (grad * accg[rows, :]).astype(BF16)
            dgu[rows, H:2 * H] = (grad * accu[rows, :]).astype(BF16)
            return 0

        lax.fori_loop(0, 2 * HR // 16, body, 0)

    def part_copy(k, d):
        return pltpu.make_async_remote_copy(
            src_ref=part.at[k, d, pl.ds(pl.multiple_of(other * R2, 16), R2), :],
            dst_ref=part_in.at[k, d],
            send_sem=part_s.at[k, d], recv_sem=part_r.at[k, d],
            device_id=pairdev, device_id_type=MESH,
        )

    def own_part(k, d):
        return part.at[k, d, pl.ds(pl.multiple_of(g * R2, 16), R2), :]

    def down(k):
        for d in range(2):
            t = snake((p + (1 + k if d else T - 1 - k)) % T, T)

            def body(n, _, d=d, t=t):
                part[k, d, :, lanes(n * WN, WN)] = jnp.dot(
                    act[d * HR:(d + 1) * HR, :], wdv[:, lanes(t * W + n * WN, WN)],
                    preferred_element_type=F32,
                ).astype(BF16)
                return 0

            lax.fori_loop(0, W // WN, body, 0)
            part_copy(k, d).start()

    def grad_act(h):
        pair_arrive(1, h)

        def body(i, _):
            d = i // (H // HN)
            n = i % (H // HN)
            off = d * h + (1 - d) * (T - h)
            t = snake((p + off) % T, T)
            ga[rows_of(d), lanes(n * HN, HN)] += lax.dot_general(
                X[1, t, rows_of(d), :], wdv[pl.ds(pl.multiple_of(n * HN, 16), HN), lanes(t * W, W)],
                (((1,), (1,)), ((), ())), preferred_element_type=F32,
            )
            return 0

        lax.fori_loop(0, 2 * (H // HN), body, 0)

    FT = tile_of(H, 512)

    def score_down(t):
        def body(i, _):
            f = i // (W // WN)
            n = i % (W // WN)
            fr = pl.ds(pl.multiple_of(f * FT, 16), FT)
            grad = jnp.dot(
                act_t[fr, :], X[1, t, :, lanes(n * WN, WN)], preferred_element_type=F32
            )
            value = jnp.abs(grad * wdv[fr, lanes(t * W + n * WN, WN)].astype(F32))
            total = imp_dn[fr, :]
            for q in range(WN // 128):
                total += value[:, q * 128:(q + 1) * 128]
            imp_dn[fr, :] = total
            return 0

        lax.fori_loop(0, (H // FT) * (W // WN), body, 0)

    NU = D // KB

    def score_gate_up(first, last):
        def body(j, _):
            slot = j % 2

            @pl.when(j + 1 < NU)
            def _():
                for c in grad_copies(j + 1, 1 - slot):
                    c.start()

            for c in grad_copies(j, slot):
                c.wait()
            for q in range(KB // 128):
                xt[q * 128:(q + 1) * 128, :] = X[0, j // NK, :, lanes((j % NK) * KB + q * 128, 128)].T
            for m in range(2):
                for n in range(H // HN):
                    grad = jnp.dot(
                        xt[...], dgu[:, m * H + n * HN:m * H + (n + 1) * HN],
                        preferred_element_type=F32,
                    )
                    value = jnp.abs(grad * wbuf[slot, m, :, n * HN:(n + 1) * HN].astype(F32))
                    imp_gu[:, n * HN:(n + 1) * HN] += jnp.sum(value.reshape(KB // 8, 8, HN), axis=0)
            return 0

        lax.fori_loop(first, last, body, 0)

    def sum_copy(k, d):
        return pltpu.make_async_remote_copy(
            src_ref=own_part(k, d), dst_ref=sum_in.at[k, d],
            send_sem=sum_s.at[k, d], recv_sem=sum_r.at[k, d],
            device_id=ringdev(d), device_id_type=MESH,
        )

    def back_rows(k):
        return part.at[T - 1, k % 2, pl.ds(pl.multiple_of(g * R2 + (k // 2) * C, 16), C), :]

    def back_copy(k):
        return pltpu.make_async_remote_copy(
            src_ref=back_rows(k), dst_ref=back.at[s],
            send_sem=back_s.at[k], recv_sem=back_r.at[k],
            device_id={"tok": (s + E - k) % E}, device_id_type=MESH,
        )

    def back_own():
        return pltpu.make_async_copy(back_rows(0), back.at[s], back_r.at[0])

    def reduce_step(k):
        for d in range(2):
            part_copy(k, d).wait_recv()
            if k > 0:
                sum_copy(k - 1, d).wait_recv()

            def body(i, _, d=d):
                rows = pl.ds(pl.multiple_of(g * R2 + i * 16, 16), 16)
                here = pl.ds(pl.multiple_of(i * 16, 16), 16)
                total = part[k, d, rows, :].astype(F32) + part_in[k, d, here, :].astype(F32)
                if k > 0:
                    total += sum_in[k - 1, d, here, :].astype(F32)
                part[k, d, rows, :] = total.astype(BF16)
                return 0

            lax.fori_loop(0, R2 // 16, body, 0)
            if k < T - 1:
                sum_copy(k, d).start()
        if k == T - 1:
            back_own().start()
            for q in range(1, E):
                back_copy(q).start()

    for ref in (accg, accu, ga):
        zero(ref)
    imp_gu[...] = jnp.zeros(imp_gu.shape, F32)
    imp_dn[...] = jnp.zeros(imp_dn.shape, F32)

    arrive(0, 0)
    for h in range(1, T):
        arrive(0, h)
        forward(h - 1)
        if h == 1:
            arrive(1, 0)
    forward(T - 1)
    for c in grad_copies(0, 0):
        c.start()
    activate()
    wd_copy().wait()
    for h in range(1, T):
        down(h - 1)
        arrive(1, h)
        grad_act(h - 1)
        if h == 1:
            score_down(tp)
        if h - 1 == T // 2:
            score_down(slice_at(T // 2, 0))
        if h == T - 1:
            down(T - 1)
        if h > 1:
            reduce_step(h - 2)
    grad_act(T - 1)
    reduce_step(T - 2)
    if T - 1 == T // 2:
        score_down(slice_at(T // 2, 0))
    gradients()
    score_gate_up(0, NU // 2)
    reduce_step(T - 1)
    score_gate_up(NU // 2, NU)
    for h in range(1, T):
        if h != T // 2:
            score_down(slice_at(h, 0))

    back_own().wait()
    for k in range(1, E):
        back_copy(k).wait()
        for a in range(2):
            a2a_copy(a, k).wait_send()
    for k in range(T):
        for d in range(2):
            part_copy(k, d).wait_send()
            if k < T - 1:
                sum_copy(k, d).wait_send()
            for a in range(2):
                for c in range(NC):
                    pair_copy(a, k, d, c).wait_send()
                    if k < T - 1:
                        ring_copy(a, k, d, c).wait_send()


def expert_call(block_rows, block_cot, w_gate, w_up, w_down):
    E, C, W = block_rows.shape
    T = lax.axis_size("tp")
    G = lax.axis_size("grp")
    H = w_gate.shape[2]
    D = w_gate.shape[1]
    NC = E // 2 if T <= 4 else 1
    KB = tile_of(W, 512)
    rows = G * E * C
    R2 = E // 2 * C
    dma = pltpu.SemaphoreType.DMA
    hbm = pl.BlockSpec(memory_space=pl.ANY)
    vmem = pl.BlockSpec(memory_space=pltpu.VMEM)
    return pl.pallas_call(
        functools.partial(expert_kernel, E, T, G, C, W, H, NC, KB),
        out_shape=(
            jax.ShapeDtypeStruct((E, C, W), BF16),
            jax.ShapeDtypeStruct((8, H), F32),
            jax.ShapeDtypeStruct((H, 128), F32),
        ),
        in_specs=[hbm] * 5,
        out_specs=(hbm, vmem, vmem),
        scratch_shapes=[
            pltpu.VMEM((2, T, rows, W), BF16),
            pltpu.VMEM((rows, H), F32),
            pltpu.VMEM((rows, H), F32),
            pltpu.VMEM((rows, H), F32),
            pltpu.VMEM((rows, H), BF16),
            pltpu.VMEM((H, rows), BF16),
            pltpu.VMEM((rows, 2 * H), BF16),
            pltpu.VMEM((H, D), BF16),
            pltpu.VMEM((T, 2, G * R2, W), BF16),
            pltpu.VMEM((T, 2, R2, W), BF16),
            pltpu.VMEM((T - 1, 2, R2, W), BF16),
            pltpu.VMEM((2, 2, KB, H), BF16),
            pltpu.VMEM((KB, rows), BF16),
            dma((2, E)), dma((2, E)),
            dma((2, T, 2, NC)), dma((2, T, 2, NC)),
            dma((2, T, 2, NC)), dma((2, T, 2, NC)),
            dma((T, 2)), dma((T, 2)),
            dma((T, 2)), dma((T, 2)),
            dma((E,)), dma((E,)),
            dma((2, 2)), dma,
        ],
        compiler_params=pltpu.CompilerParams(
            collective_id=0, has_side_effects=True, vmem_limit_bytes=64 * 1024 * 1024 - 65536
        ),
        cost_estimate=pl.CostEstimate(
            flops=14 * rows * D * H, bytes_accessed=6 * D * H * 2, transcendentals=rows * H
        ),
        name="expert_layer",
    )(block_rows, block_cot, w_gate, w_up, w_down)


def on_device(hidden, gain, expert_ids, gate_weights, segment_ids, upstream, w_gate, w_up, w_down):
    rows_here = hidden.shape[0]
    top_count = expert_ids.shape[1]
    experts = lax.axis_size("tok")
    groups = lax.axis_size("grp")
    capacity = -(-(5 * rows_here // (2 * experts)) // 16) * 16
    width = w_gate.shape[1]
    documents = jnp.arange(experts * groups, dtype=jnp.int32)
    doc_onehot = (segment_ids[:, None] == documents[None, :]).astype(F32)
    doc_len = lax.psum(jnp.sum(doc_onehot, axis=0), ("tok", "grp"))
    tok_len = jnp.sum(doc_onehot * doc_len[None, :], axis=1)
    tok_weight = rows_here / tok_len
    onehot = (
        expert_ids.reshape(-1)[:, None] == jnp.arange(experts, dtype=jnp.int32)[None, :]
    ).astype(jnp.int32)
    before = jnp.cumsum(onehot, axis=0) - onehot
    slot_ids = jnp.sum(before * onehot, axis=1).reshape(rows_here, top_count)
    targets = expert_ids * capacity + slot_ids
    all_slots = jnp.arange(experts * capacity, dtype=jnp.int32)
    matches = all_slots[:, None, None] == targets[None, :, :]
    placing = jnp.any(matches, axis=2).astype(BF16)
    scaled = gate_weights * tok_weight[:, None]
    slot_scale = jnp.sum(jnp.where(matches, scaled[None, :, :], 0.0), axis=(1, 2))
    wide_hidden = hidden.astype(F32)
    squares = lax.psum(jnp.sum(wide_hidden * wide_hidden, axis=1), "tp")
    scaling = lax.rsqrt(squares / width + 1e-05)
    normed = (wide_hidden * scaling[:, None] * gain.astype(F32)[None, :]).astype(BF16)
    block_rows = jnp.dot(placing, normed, preferred_element_type=F32).astype(BF16)
    block_cot = jnp.dot(placing, upstream, preferred_element_type=F32) * slot_scale[:, None]
    block_rows = block_rows.reshape(experts, capacity, -1)
    block_cot = block_cot.astype(BF16).reshape(experts, capacity, -1)
    back, imp_gu, imp_dn = expert_call(block_rows, block_cot, w_gate, w_up, w_down)
    scores = jnp.sum(imp_gu, axis=0) + jnp.sum(imp_dn, axis=1)
    importance = scores / (rows_here * experts * groups)
    returned = back.reshape(experts * capacity, -1)
    combined = jnp.zeros(hidden.shape, F32)
    for k in range(top_count):
        pick = (targets[:, k][:, None] == all_slots[None, :]).astype(BF16)
        combined += gate_weights[:, k][:, None] * jnp.dot(pick, returned, preferred_element_type=F32)
    mixed = (wide_hidden + combined).astype(BF16)
    return (mixed, importance[None, :])


def solution(mesh):
    placed = (
        P(("tok", "grp"), "tp"),
        P("tp"),
        P(("tok", "grp"), None),
        P(("tok", "grp"), None),
        P(("tok", "grp")),
        P(("tok", "grp"), "tp"),
        P("tok", None, ("tp", "grp")),
        P("tok", None, ("tp", "grp")),
        P("tok", ("tp", "grp"), None),
    )
    return jax.shard_map(
        on_device,
        mesh=mesh,
        in_specs=placed,
        out_specs=(P(("tok", "grp"), "tp"), P("tok", ("tp", "grp"))),
        check_vma=False,
    )
```

time: 372 us -> 221 us (0.59)
  the two profiles are of different devices: /device:TPU:0 before, /device:TPU:10 now
where the time goes in v1:
time: 221 us; the launch traced here: 220 us
  Pallas kernels  182 us (82%)
  blocking collectives  21.1 us (10%)
  matrix products  6.71 us (3%)
  other arithmetic  6.13 us (3%)
  local copies, waits for them, and re-layouts  3.18 us (1%)
    pallas_call x1, Pallas kernels, expert_call(): pl.pallas_call(functools.partial(expert_kernel, E, T, G, C, W, H, NC, KB)...  182 us
    psum x1, blocking collectives, on_device(): doc_len = lax.psum(jnp.sum(doc_onehot, axis=0), ('tok', 'grp'))  13 us
    psum x1, blocking collectives, on_device(): squares = lax.psum(jnp.sum(wide_hidden * wide_hidden, axis=1), 'tp')  8.06 us

profile of v1, /device:TPU:10, one launch (start us, length us, event | category | flops | bytes accessed | tf_op | source)
XLA Modules:
  0.0 219.9 jit_solution(7933430108732913251)
XLA Ops:
  0.6 0.0 copy-start.1
  0.6 0.8 copy.36
  1.5 0.1 eq.85
  1.6 1.2 reduce-window.6
  2.9 0.1 slice.24
  2.9 0.1 copy.38
  3.1 0.1 copy.39
  3.2 0.1 add_bitcast_fusion
  3.2 0.1 eq.81
  3.4 0.1 reshape.61
  3.6 0.1 copy.40
  3.6 0.7 multiply_add_fusion
  4.3 0.0 copy-start.5
  4.4 0.8 convert_reduce_fusion
  5.1 13.0 %psum.15 = f32[8]{0:T(128)S(1)} all-reduce(f32[8]{0:T(128)S(1)} %convert_reduce_fusion), channel_id=1, replica_groups=mesh['tok'=4,'tp'=4,'grp'=2] {'tok','grp'}, use_global_device_ids=true, to_apply=%region_7.8 | all-reduce | flops 8 | bytes 64 | tf_op jit(solution)/shard_map/psum | solution.py:474
  18.2 0.7 select_reduce_fusion.1
  18.9 0.7 broadcast_multiply_fusion
  19.6 0.1 select_reduce_fusion
  19.7 2.4 %fusion = bf16[320,1536]{1,0:T(8,128)(2,1)} fusion(pred[320,128]{1,0:T(8,128)(4,1)S(1)} %fusion.10, bf16[128,1536]{1,0:T(8,128)(2,1)} %param.14, f32[320]{0:T(512)S(1)} %select_reduce_fusion), kind=kOutput, calls=%fused_computation.1 | convolution fusion | flops 126812160 | bytes 1418496 | tf_op jit(solution)/shard_map/dot_general | solution.py:493
  22.1 0.0 copy-done.5
  22.1 0.7 convert_element_type.34
  22.8 0.0 copy-done.1
  22.8 0.2 fusion.4
  23.0 8.1 %psum.14 = f32[128]{0:T(128)S(1)} all-reduce(f32[128]{0:T(128)S(1)} %fusion.4), channel_id=1, replica_groups=mesh['tok'=4,'tp'=4,'grp'=2] {'tp'}, use_global_device_ids=true, to_apply=%region_5.6 | all-reduce | flops 128 | bytes 1024 | tf_op jit(solution)/shard_map/psum | solution.py:489
  31.1 1.5 convolution_convert_fusion
  32.5 182.0 %expert_layer.1 = (bf16[4,80,1536]{2,1,0:T(8,128)(2,1)}, f32[8,1024]{1,0:T(8,128)}, f32[1024,128]{1,0:T(8,128)}) custom-call(bf16[4,80,1536]{2,1,0:T(8,128)(2,1)} %bitcast.39, bf16[4,80,1536]{2,1,0:T(8,128)(2,1)} %bitcast.38, bf16[1,6144,1024]{2,1,0:T(8,128)(2,1)} %wg.1, bf16[1,6144,1024]{2,1,0:T(8,128)(2,1)} %wu.1, bf16[1,1024,6144]{2,1,0:T(8,128)(2,1)} %wd.1), custom_call_target="tpu_custom_call" | custom-call | flops 56371445760 | bytes 75497472 | tf_op jit(solution)/shard_map/expert_layer/pallas_call | solution.py:424
  214.6 0.0 copy-start
  214.6 0.0 copy-start.2
  214.6 0.8 slice_bitcast_fusion
  215.4 0.8 slice_bitcast_fusion.1
  216.1 0.0 copy-start.4
  216.1 0.0 copy-start.3
  216.1 1.7 convolution_multiply_fusion.2
  217.8 0.0 copy-done
  217.8 0.0 copy-done.2
  217.9 1.2 fusion.3
  219.0 0.0 copy-done.4
  219.0 0.0 copy-done.3
  219.1 0.2 reduce_sum.69
  219.3 0.6 add_multiply_fusion
  (8 shorter events, 0.1 us)
Async XLA Ops:
  0.6 22.2 %copy-start.1 = (bf16[128,1536]{1,0:T(8,128)(2,1)S(1)}, bf16[128,1536]{1,0:T(8,128)(2,1)}, u32[]{:S(2)}) copy-start(bf16[128,1536]{1,0:T(8,128)(2,1)} %param.9) | copy-start | bytes 1179652
  4.3 17.8 %copy-start.5 = (s32[128,2]{0,1:T(2,128)}, s32[128,2]{0,1:T(2,128)S(1)}, u32[]{:S(2)}) copy-start(s32[128,2]{0,1:T(2,128)S(1)} %multiply_add_fusion) | copy-start | bytes 3076
  214.6 3.3 %copy-start = (bf16[4,80,1536]{2,1,0:T(8,128)(2,1)S(1)}, bf16[4,80,1536]{2,1,0:T(8,128)(2,1)}, u32[]{:S(2)}) copy-start(bf16[4,80,1536]{2,1,0:T(8,128)(2,1)} %get-tuple-element.5) | copy-start | bytes 2949124
  214.6 3.3 %copy-start.2 = (bf16[128,1536]{1,0:T(8,128)(2,1)S(1)}, bf16[128,1536]{1,0:T(8,128)(2,1)}, u32[]{:S(2)}) copy-start(bf16[128,1536]{1,0:T(8,128)(2,1)} %param.9) | copy-start | bytes 1179652
  216.1 2.9 %copy-start.4 = (f32[8,1024]{1,0:T(8,128)S(1)}, f32[8,1024]{1,0:T(8,128)}, u32[]{:S(2)}) copy-start(f32[8,1024]{1,0:T(8,128)} %get-tuple-element.6) | copy-start | bytes 98308
  216.1 2.9 %copy-start.3 = (f32[1024,128]{1,0:T(8,128)S(1)}, f32[1024,128]{1,0:T(8,128)}, u32[]{:S(2)}) copy-start(f32[1024,128]{1,0:T(8,128)} %get-tuple-element.7) | copy-start | bytes 1572868

commit v2 on v1

--- a/solution.py
+++ b/solution.py
@@ -28,10 +28,12 @@
 
 def expert_kernel(
     E, T, G, C, W, H, NC, KB,
-    blk_rows, blk_cot, wg, wu, wd,
-    back, imp_gu, imp_dn,
+    hidden, gain, upstream, placing, placed_gates, docs, picks, wg, wu, wd,
+    mixed, imp,
     X, accg, accu, ga, act, act_t, dgu, wdv, part, part_in, sum_in, wbuf, xt,
+    imp_gu, imp_dn, back, sq, doc,
     a2a_s, a2a_r, ring_s, ring_r, pair_s, pair_r, part_s, part_r, sum_s, sum_r, back_s, back_r, wsem, wdsem,
+    sq_s, sq_r, doc_s, doc_r,
 ):
     s = lax.axis_index("tok")
     tp = lax.axis_index("tp")
@@ -46,7 +48,7 @@
     CR = R2 // NC
     D = T * W
     NK = W // KB
-    blks = (blk_rows, blk_cot)
+    N = hidden.shape[0]
 
     def tokdev(k):
         return {"tok": (s + k) % E}
@@ -59,8 +61,11 @@
     barrier = pltpu.get_barrier_semaphore()
     for k in range(1, E):
         pl.semaphore_signal(barrier, inc=1, device_id=tokdev(k), device_id_type=MESH)
-    for d in range(2):
-        pl.semaphore_signal(barrier, inc=1, device_id=ringdev(d), device_id_type=MESH)
+        pl.semaphore_signal(
+            barrier, inc=1, device_id={"tok": (s + k) % E, "grp": other}, device_id_type=MESH
+        )
+    for k in range(1, T):
+        pl.semaphore_signal(barrier, inc=1, device_id={"tp": (tp + k) % T}, device_id_type=MESH)
     pl.semaphore_signal(barrier, inc=1, device_id=pairdev, device_id_type=MESH)
 
     def wd_copy():
@@ -92,9 +97,12 @@
     def group_rows(half, grp, c, n):
         return pl.ds(pl.multiple_of(half * HR + grp * R2 + c * n, 16), n)
 
+    def block(a, e):
+        return part.at[T - 1, a, pl.ds(pl.multiple_of(e * C, 16), C), :]
+
     def a2a_copy(a, k):
         return pltpu.make_async_remote_copy(
-            src_ref=blks[a].at[(s + k) % E],
+            src_ref=block(a, (s + k) % E),
             dst_ref=X.at[a, tp, group_rows(k % 2, g, k // 2, C), :],
             send_sem=a2a_s.at[a, k], recv_sem=a2a_r.at[a, k],
             device_id=tokdev(k), device_id_type=MESH,
@@ -102,7 +110,7 @@
 
     def own_copy(a):
         return pltpu.make_async_copy(
-            blks[a].at[s], X.at[a, tp, group_rows(0, g, 0, C), :], a2a_r.at[a, 0]
+            block(a, s), X.at[a, tp, group_rows(0, g, 0, C), :], a2a_r.at[a, 0]
         )
 
     def slice_at(h, d):
@@ -124,11 +132,83 @@
             device_id=pairdev, device_id_type=MESH,
         )
 
-    pl.semaphore_wait(barrier, E + 2)
-    for a in range(2):
+    def sq_copy(k):
+        return pltpu.make_async_remote_copy(
+            src_ref=sq.at[0], dst_ref=sq.at[k], send_sem=sq_s.at[k], recv_sem=sq_r.at[k],
+            device_id={"tp": (tp + k) % T}, device_id_type=MESH,
+        )
+
+    def doc_copy(k):
+        return pltpu.make_async_remote_copy(
+            src_ref=doc.at[0], dst_ref=doc.at[k], send_sem=doc_s.at[k], recv_sem=doc_r.at[k],
+            device_id={"tok": (s + k // G) % E, "grp": (g + k % G) % G}, device_id_type=MESH,
+        )
+
+    def send_blocks(a):
         own_copy(a).start()
         for k in range(1, E):
             a2a_copy(a, k).start()
+
+    def lane_sum(value):
+        return jnp.sum(value, axis=1, keepdims=True)
+
+    def exchange_sums():
+        total = jnp.zeros((N, 128), F32)
+        for n in range(W // 128):
+            value = hidden[:, n * 128:(n + 1) * 128].astype(F32)
+            total += value * value
+        sq[0] = jnp.broadcast_to(lane_sum(total), (N, 128))
+        counts = jnp.sum(docs[...].astype(F32), axis=0, keepdims=True)
+        doc[0] = jnp.broadcast_to(counts, (8, 128))
+        pl.semaphore_wait(barrier, 2 * (E - 1) + T)
+        for k in range(1, T):
+            sq_copy(k).start()
+        for k in range(1, E * G):
+            doc_copy(k).start()
+
+    def place_rows():
+        total = sq[0]
+        for k in range(1, T):
+            sq_copy(k).wait_recv()
+            total += sq[k]
+        scaling = lax.rsqrt(total / D + 1e-05)
+        where = placing[...]
+        for n in range(W // 128):
+            cols = slice(n * 128, (n + 1) * 128)
+            normed = (hidden[:, cols].astype(F32) * scaling * gain[:, cols].astype(F32)).astype(BF16)
+            part[T - 1, 0, :, cols] = jnp.dot(where, normed, preferred_element_type=F32).astype(BF16)
+
+    def place_cot():
+        lengths = doc[0]
+        for k in range(1, E * G):
+            doc_copy(k).wait_recv()
+            lengths += doc[k]
+        where = placing[...]
+        slot_docs = jnp.dot(where, docs[...], preferred_element_type=F32)
+        slot_len = lane_sum(slot_docs * lengths[0:1, :])
+        weight = jnp.where(slot_len > 0.0, N / jnp.maximum(slot_len, 1.0), 0.0)
+        scale = lane_sum(placed_gates[...]) * weight
+        CW = tile_of(W, 256)
+        for n in range(W // CW):
+            cols = slice(n * CW, (n + 1) * CW)
+            value = jnp.dot(where, upstream[:, cols], preferred_element_type=F32)
+            part[T - 1, 1, :, cols] = (value * scale).astype(BF16)
+
+    def combine():
+        back_own().wait()
+        for k in range(1, E):
+            back_copy(k).wait_recv()
+        CW = tile_of(W, 256)
+        ways = []
+        for k in range(picks.shape[0]):
+            pick = picks[k]
+            ways.append((jnp.where(pick != 0.0, 1.0, 0.0).astype(BF16), lane_sum(pick)))
+        for n in range(W // CW):
+            cols = slice(n * CW, (n + 1) * CW)
+            total = jnp.zeros((N, CW), F32)
+            for where, gate in ways:
+                total += gate * jnp.dot(where, back[:, cols], preferred_element_type=F32)
+            mixed[:, cols] = (hidden[:, cols].astype(F32) + total).astype(BF16)
 
     def arrive(a, h):
         for c in range(NC):
@@ -320,13 +400,15 @@
 
     def back_copy(k):
         return pltpu.make_async_remote_copy(
-            src_ref=back_rows(k), dst_ref=back.at[s],
+            src_ref=back_rows(k), dst_ref=back.at[pl.ds(pl.multiple_of(s * C, 16), C), :],
             send_sem=back_s.at[k], recv_sem=back_r.at[k],
             device_id={"tok": (s + E - k) % E}, device_id_type=MESH,
         )
 
     def back_own():
-        return pltpu.make_async_copy(back_rows(0), back.at[s], back_r.at[0])
+        return pltpu.make_async_copy(
+            back_rows(0), back.at[pl.ds(pl.multiple_of(s * C, 16), C), :], back_r.at[0]
+        )
 
     def reduce_step(k):
         for d in range(2):
@@ -351,51 +433,62 @@
             for q in range(1, E):
                 back_copy(q).start()
 
+    exchange_sums()
     for ref in (accg, accu, ga):
         zero(ref)
     imp_gu[...] = jnp.zeros(imp_gu.shape, F32)
     imp_dn[...] = jnp.zeros(imp_dn.shape, F32)
+    place_rows()
+    send_blocks(0)
+    place_cot()
 
     arrive(0, 0)
+    send_blocks(1)
     for h in range(1, T):
         arrive(0, h)
         forward(h - 1)
-        if h == 1:
+        if h == min(2, T - 1):
             arrive(1, 0)
     forward(T - 1)
     for c in grad_copies(0, 0):
         c.start()
     activate()
     wd_copy().wait()
+    for a in range(2):
+        for k in range(1, E):
+            a2a_copy(a, k).wait_send()
     for h in range(1, T):
         down(h - 1)
+        if h > 1:
+            reduce_step(h - 2)
         arrive(1, h)
         grad_act(h - 1)
         if h == 1:
             score_down(tp)
-        if h - 1 == T // 2:
-            score_down(slice_at(T // 2, 0))
-        if h == T - 1:
-            down(T - 1)
-        if h > 1:
-            reduce_step(h - 2)
+    down(T - 1)
     grad_act(T - 1)
+    gradients()
+    first, second = NU // 4, NU // 4 + NU // 3
+    score_gate_up(0, first)
     reduce_step(T - 2)
-    if T - 1 == T // 2:
-        score_down(slice_at(T // 2, 0))
-    gradients()
-    score_gate_up(0, NU // 2)
+    score_gate_up(first, second)
     reduce_step(T - 1)
-    score_gate_up(NU // 2, NU)
+    score_gate_up(second, NU)
     for h in range(1, T):
-        if h != T // 2:
-            score_down(slice_at(h, 0))
-
-    back_own().wait()
+        score_down(slice_at(h, 0))
+    for n in range(H // 128):
+        cols = slice(n * 128, (n + 1) * 128)
+        value = jnp.sum(imp_gu[:, cols], axis=0, keepdims=True)
+        value += jnp.sum(imp_dn[cols, :].T, axis=0, keepdims=True)
+        imp[:, cols] = value / (N * E * G)
+    combine()
+
     for k in range(1, E):
-        back_copy(k).wait()
-        for a in range(2):
-            a2a_copy(a, k).wait_send()
+        back_copy(k).wait_send()
+    for k in range(1, T):
+        sq_copy(k).wait_send()
+    for k in range(1, E * G):
+        doc_copy(k).wait_send()
     for k in range(T):
         for d in range(2):
             part_copy(k, d).wait_send()
@@ -408,8 +501,10 @@
                         ring_copy(a, k, d, c).wait_send()
 
 
-def expert_call(block_rows, block_cot, w_gate, w_up, w_down):
-    E, C, W = block_rows.shape
+def expert_call(hidden, gain, upstream, placing, placed_gates, docs, picks, w_gate, w_up, w_down):
+    N, W = hidden.shape
+    E = lax.axis_size("tok")
+    C = placing.shape[0] // E
     T = lax.axis_size("tp")
     G = lax.axis_size("grp")
     H = w_gate.shape[2]
@@ -424,12 +519,11 @@
     return pl.pallas_call(
         functools.partial(expert_kernel, E, T, G, C, W, H, NC, KB),
         out_shape=(
-            jax.ShapeDtypeStruct((E, C, W), BF16),
-            jax.ShapeDtypeStruct((8, H), F32),
-            jax.ShapeDtypeStruct((H, 128), F32),
+            jax.ShapeDtypeStruct((N, W), BF16),
+            jax.ShapeDtypeStruct((1, H), F32),
         ),
-        in_specs=[hbm] * 5,
-        out_specs=(hbm, vmem, vmem),
+        in_specs=[vmem] * 7 + [hbm] * 3,
+        out_specs=(vmem, vmem),
         scratch_shapes=[
             pltpu.VMEM((2, T, rows, W), BF16),
             pltpu.VMEM((rows, H), F32),
@@ -444,6 +538,11 @@
             pltpu.VMEM((T - 1, 2, R2, W), BF16),
             pltpu.VMEM((2, 2, KB, H), BF16),
             pltpu.VMEM((KB, rows), BF16),
+            pltpu.VMEM((8, H), F32),
+            pltpu.VMEM((H, 128), F32),
+            pltpu.VMEM((E * C, W), BF16),
+            pltpu.VMEM((T, N, 128), F32),
+            pltpu.VMEM((E * G, 8, 128), F32),
             dma((2, E)), dma((2, E)),
             dma((2, T, 2, NC)), dma((2, T, 2, NC)),
             dma((2, T, 2, NC)), dma((2, T, 2, NC)),
@@ -451,6 +550,7 @@
             dma((T, 2)), dma((T, 2)),
             dma((E,)), dma((E,)),
             dma((2, 2)), dma,
+            dma((T,)), dma((T,)), dma((E * G,)), dma((E * G,)),
         ],
         compiler_params=pltpu.CompilerParams(
             collective_id=0, has_side_effects=True, vmem_limit_bytes=64 * 1024 * 1024 - 65536
@@ -459,7 +559,7 @@
             flops=14 * rows * D * H, bytes_accessed=6 * D * H * 2, transcendentals=rows * H
         ),
         name="expert_layer",
-    )(block_rows, block_cot, w_gate, w_up, w_down)
+    )(hidden, gain, upstream, placing, placed_gates, docs, picks, w_gate, w_up, w_down)
 
 
 def on_device(hidden, gain, expert_ids, gate_weights, segment_ids, upstream, w_gate, w_up, w_down):
@@ -469,40 +569,27 @@
     groups = lax.axis_size("grp")
     capacity = -(-(5 * rows_here // (2 * experts)) // 16) * 16
     width = w_gate.shape[1]
-    documents = jnp.arange(experts * groups, dtype=jnp.int32)
-    doc_onehot = (segment_ids[:, None] == documents[None, :]).astype(F32)
-    doc_len = lax.psum(jnp.sum(doc_onehot, axis=0), ("tok", "grp"))
-    tok_len = jnp.sum(doc_onehot * doc_len[None, :], axis=1)
-    tok_weight = rows_here / tok_len
-    onehot = (
-        expert_ids.reshape(-1)[:, None] == jnp.arange(experts, dtype=jnp.int32)[None, :]
-    ).astype(jnp.int32)
-    before = jnp.cumsum(onehot, axis=0) - onehot
-    slot_ids = jnp.sum(before * onehot, axis=1).reshape(rows_here, top_count)
-    targets = expert_ids * capacity + slot_ids
+    places = jnp.arange(rows_here, dtype=jnp.int32)
+    earlier = places[None, :] < places[:, None]
     all_slots = jnp.arange(experts * capacity, dtype=jnp.int32)
-    matches = all_slots[:, None, None] == targets[None, :, :]
-    placing = jnp.any(matches, axis=2).astype(BF16)
-    scaled = gate_weights * tok_weight[:, None]
-    slot_scale = jnp.sum(jnp.where(matches, scaled[None, :, :], 0.0), axis=(1, 2))
-    wide_hidden = hidden.astype(F32)
-    squares = lax.psum(jnp.sum(wide_hidden * wide_hidden, axis=1), "tp")
-    scaling = lax.rsqrt(squares / width + 1e-05)
-    normed = (wide_hidden * scaling[:, None] * gain.astype(F32)[None, :]).astype(BF16)
-    block_rows = jnp.dot(placing, normed, preferred_element_type=F32).astype(BF16)
-    block_cot = jnp.dot(placing, upstream, preferred_element_type=F32) * slot_scale[:, None]
-    block_rows = block_rows.reshape(experts, capacity, -1)
-    block_cot = block_cot.astype(BF16).reshape(experts, capacity, -1)
-    back, imp_gu, imp_dn = expert_call(block_rows, block_cot, w_gate, w_up, w_down)
-    scores = jnp.sum(imp_gu, axis=0) + jnp.sum(imp_dn, axis=1)
-    importance = scores / (rows_here * experts * groups)
-    returned = back.reshape(experts * capacity, -1)
-    combined = jnp.zeros(hidden.shape, F32)
+    docs = (segment_ids[:, None] == jnp.arange(128, dtype=jnp.int32)[None, :]).astype(BF16)
+    placed_gates = jnp.zeros((experts * capacity, rows_here), F32)
+    placing = jnp.zeros((experts * capacity, rows_here), jnp.bool_)
+    picks = []
     for k in range(top_count):
-        pick = (targets[:, k][:, None] == all_slots[None, :]).astype(BF16)
-        combined += gate_weights[:, k][:, None] * jnp.dot(pick, returned, preferred_element_type=F32)
-    mixed = (wide_hidden + combined).astype(BF16)
-    return (mixed, importance[None, :])
+        same = jnp.zeros((rows_here, rows_here), jnp.bool_)
+        for other in range(top_count):
+            same |= expert_ids[:, k][:, None] == expert_ids[:, other][None, :]
+        slot = jnp.sum((same & earlier).astype(jnp.int32), axis=1)
+        target = expert_ids[:, k] * capacity + slot
+        match = all_slots[:, None] == target[None, :]
+        placing |= match
+        placed_gates += jnp.where(match, gate_weights[:, k][None, :], 0.0)
+        picks.append(jnp.where(target[:, None] == all_slots[None, :], gate_weights[:, k][:, None], 0.0))
+    return expert_call(
+        hidden, gain[None, :], upstream, placing.astype(BF16), placed_gates, docs, jnp.stack(picks),
+        w_gate, w_up, w_down,
+    )
 
 
 def solution(mesh):

time: 221 us -> 192 us (0.87)
  the two profiles are of different devices: /device:TPU:10 before, /device:TPU:26 now
where the time goes in v2:
time: 192 us; the launch traced here: 191 us
  Pallas kernels  179 us (93%)
  local copies, waits for them, and re-layouts  5.84 us (3%)
  other arithmetic  5.31 us (3%)
    pallas_call x1, Pallas kernels, expert_call(): pl.pallas_call(functools.partial(expert_kernel, E, T, G, C, W, H, NC, KB)...  179 us

profile of v2, /device:TPU:26, one launch (start us, length us, event | category | flops | bytes accessed | tf_op | source)
XLA Modules:
  0.0 191.2 jit_solution(257990024547657320)
XLA Ops:
  0.6 0.8 slice_bitcast_fusion.1
  1.4 0.8 slice_bitcast_fusion.3
  2.1 0.2 convert_reduce_fusion.1
  2.3 0.8 fusion.8
  3.1 0.8 multiply_add_fusion.1
  3.9 1.3 broadcast_in_dim.55.gain
  5.1 1.3 fusion.6.docs
  6.5 0.7 fusion.3.placing
  7.1 0.7 select_add_fusion.placed_gates
  7.8 0.1 fusion
  8.0 0.8 pad_maximum_fusion.picks
  8.8 179.4 %expert_layer.1 = (bf16[128,1536]{1,0:T(8,128)(2,1)}, f32[1,1024]{1,0:T(1,128)}) custom-call(bf16[128,1536]{1,0:T(8,128)(2,1)} %hidden.1, bf16[1,1536]{1,0:T(2,128)(2,1)} %broadcast_in_dim.55.gain, bf16[128,1536]{1,0:T(8,128)(2,1)} %upstream.1, bf16[320,128]{1,0:T(8,128)(2,1)} %fusion.3.placing, f32[320,128]{1,0:T(8,128)} %select_add_fusion.placed_gates, ...), custom_call_target="tpu_custom_call" | custom-call | flops 56371445760 | bytes 75497472 | tf_op jit(solution)/shard_map/expert_layer/pallas_call | solution.py:519
  188.1 1.8 copy.13
  189.9 1.3 copy.14

commit v3 on v2

--- a/solution.py
+++ b/solution.py
@@ -32,7 +32,7 @@
     mixed, imp,
     X, accg, accu, ga, act, act_t, dgu, wdv, part, part_in, sum_in, wbuf, xt,
     imp_gu, imp_dn, back, sq, doc,
-    a2a_s, a2a_r, ring_s, ring_r, pair_s, pair_r, part_s, part_r, sum_s, sum_r, back_s, back_r, wsem, wdsem,
+    a2a_s, a2a_r, ring_s, ring_r, pair_s, pair_r, part_s, part_r, sum_s, sum_r, back_s, back_r, wsem, gsem, wdsem,
     sq_s, sq_r, doc_s, doc_r,
 ):
     s = lax.axis_index("tok")
@@ -42,13 +42,17 @@
     right = snake((p + 1) % T, T)
     left = snake((p + T - 1) % T, T)
     other = 1 - g
-    E2 = E // 2
-    R2 = E2 * C
-    HR = G * R2
-    CR = R2 // NC
+    R = E * C
+    CR = R // NC
     D = T * W
     NK = W // KB
     N = hidden.shape[0]
+    W0 = -(-W // 256) * 128
+    LOW = (0, W0)
+    WIDE = (W0, W - W0)
+
+    def part_lanes(d):
+        return slice(LOW[d], LOW[d] + WIDE[d])
 
     def tokdev(k):
         return {"tok": (s + k) % E}
@@ -68,56 +72,55 @@
         pl.semaphore_signal(barrier, inc=1, device_id={"tp": (tp + k) % T}, device_id_type=MESH)
     pl.semaphore_signal(barrier, inc=1, device_id=pairdev, device_id_type=MESH)
 
+    def slice_at(h, d):
+        return snake((p + (h if d else T - h)) % T, T)
+
     def wd_copy():
         return pltpu.make_async_copy(wd.at[0], wdv, wdsem)
 
-    def fwd_copies(i, slot):
-        h = i // (2 * NK)
-        d = (i // NK) % 2
-        k = i % NK
-        off = d * h + (1 - d) * (T - h)
-        t = snake((p + off) % T, T)
-        start = pl.multiple_of(t * W + k * KB, KB)
-        return [
-            pltpu.make_async_copy(w.at[0, pl.ds(start, KB), :], wbuf.at[slot, m], wsem.at[slot, m])
-            for m, w in enumerate((wg, wu))
-        ]
+    def fwd_copy(u):
+        h, d, m = u // 4, u // 2 % 2, u % 2
+        start = pl.multiple_of(slice_at(h, d) * W + LOW[d], 128)
+        return pltpu.make_async_copy(
+            (wg, wu)[m].at[0, pl.ds(start, WIDE[d]), :],
+            wbuf.at[pl.ds(u % 3 * W0, WIDE[d]), :], wsem.at[u % 3],
+        )
 
     def grad_copies(j, slot):
         start = pl.multiple_of(j * KB, KB)
         return [
-            pltpu.make_async_copy(w.at[0, pl.ds(start, KB), :], wbuf.at[slot, m], wsem.at[slot, m])
+            pltpu.make_async_copy(
+                w.at[0, pl.ds(start, KB), :],
+                wbuf.at[pl.ds(pl.multiple_of((slot * 2 + m) * KB, KB), KB), :], gsem.at[slot, m],
+            )
             for m, w in enumerate((wg, wu))
         ]
 
-    for c in fwd_copies(0, 0):
-        c.start()
+    for u in range(3):
+        fwd_copy(u).start()
     wd_copy().start()
 
-    def group_rows(half, grp, c, n):
-        return pl.ds(pl.multiple_of(half * HR + grp * R2 + c * n, 16), n)
+    def group_rows(grp, c, n):
+        return pl.ds(pl.multiple_of(grp * R + c * n, 16), n)
 
     def block(a, e):
-        return part.at[T - 1, a, pl.ds(pl.multiple_of(e * C, 16), C), :]
+        return part.at[T - 1, pl.ds(pl.multiple_of(a * R + e * C, 16), C), :]
 
     def a2a_copy(a, k):
         return pltpu.make_async_remote_copy(
             src_ref=block(a, (s + k) % E),
-            dst_ref=X.at[a, tp, group_rows(k % 2, g, k // 2, C), :],
+            dst_ref=X.at[a, tp, group_rows(g, k, C), :],
             send_sem=a2a_s.at[a, k], recv_sem=a2a_r.at[a, k],
             device_id=tokdev(k), device_id_type=MESH,
         )
 
     def own_copy(a):
         return pltpu.make_async_copy(
-            block(a, s), X.at[a, tp, group_rows(0, g, 0, C), :], a2a_r.at[a, 0]
-        )
-
-    def slice_at(h, d):
-        return snake((p + (h if d else T - h)) % T, T)
+            block(a, s), X.at[a, tp, group_rows(g, 0, C), :], a2a_r.at[a, 0]
+        )
 
     def ring_copy(a, h, d, c, received=False):
-        view = X.at[a, slice_at(h + 1 if received else h, d), group_rows(d, g, c, CR), :]
+        view = X.at[a, slice_at(h + 1 if received else h, d), group_rows(g, c, CR), part_lanes(d)]
         return pltpu.make_async_remote_copy(
             src_ref=view, dst_ref=view,
             send_sem=ring_s.at[a, h, d, c], recv_sem=ring_r.at[a, h, d, c],
@@ -125,7 +128,7 @@
         )
 
     def pair_copy(a, h, d, c, received=False):
-        view = X.at[a, slice_at(h, d), group_rows(d, other if received else g, c, CR), :]
+        view = X.at[a, slice_at(h, d), group_rows(other if received else g, c, CR), part_lanes(d)]
         return pltpu.make_async_remote_copy(
             src_ref=view, dst_ref=view,
             send_sem=pair_s.at[a, h, d, c], recv_sem=pair_r.at[a, h, d, c],
@@ -176,7 +179,7 @@
         for n in range(W // 128):
             cols = slice(n * 128, (n + 1) * 128)
             normed = (hidden[:, cols].astype(F32) * scaling * gain[:, cols].astype(F32)).astype(BF16)
-            part[T - 1, 0, :, cols] = jnp.dot(where, normed, preferred_element_type=F32).astype(BF16)
+            part[T - 1, 0:R, cols] = jnp.dot(where, normed, preferred_element_type=F32).astype(BF16)
 
     def place_cot():
         lengths = doc[0]
@@ -192,7 +195,7 @@
         for n in range(W // CW):
             cols = slice(n * CW, (n + 1) * CW)
             value = jnp.dot(where, upstream[:, cols], preferred_element_type=F32)
-            part[T - 1, 1, :, cols] = (value * scale).astype(BF16)
+            part[T - 1, R:2 * R, cols] = (value * scale).astype(BF16)
 
     def combine():
         back_own().wait()
@@ -214,9 +217,8 @@
         for c in range(NC):
             for d in range(2):
                 if h == 0:
-                    per = E2 // NC
-                    for q in range(c * per, (c + 1) * per):
-                        k = 2 * q + d
+                    per = E // NC
+                    for k in range(c * per, (c + 1) * per) if d == 0 else ():
                         if k == 0:
                             own_copy(a).wait()
                         else:
@@ -232,14 +234,10 @@
             for d in range(2):
                 pair_copy(a, h, d, c, True).wait_recv()
 
-    def rows_of(d):
-        return pl.ds(pl.multiple_of(d * HR, 16), HR)
-
     def lanes(start, n, unit=128):
         return pl.ds(pl.multiple_of(start, unit), n)
 
     HN = tile_of(H, 256)
-    WN = tile_of(W, 256)
 
     def zero(ref):
         def body(i, _):
@@ -250,30 +248,22 @@
     def forward(h):
         pair_arrive(0, h)
 
-        def body(i, _):
-            slot = i % 2
-
-            @pl.when(i + 1 < T * 2 * NK)
-            def _():
-                for c in fwd_copies(i + 1, 1 - slot):
-                    c.start()
-
-            for c in fwd_copies(i, slot):
-                c.wait()
-            d = (i // NK) % 2
-            k = i % NK
-            off = d * h + (1 - d) * (T - h)
-            t = snake((p + off) % T, T)
-            x = X[0, t, rows_of(d), lanes(k * KB, KB)]
-            for m, acc in enumerate((accg, accu)):
-                for n in range(H // HN):
-                    cols = slice(n * HN, (n + 1) * HN)
-                    acc[rows_of(d), cols] += jnp.dot(
-                        x, wbuf[slot, m, :, cols], preferred_element_type=F32
-                    )
-            return 0
-
-        lax.fori_loop(h * 2 * NK, (h + 1) * 2 * NK, body, 0)
+        for u in range(4 * h, 4 * h + 4):
+            d, acc = u // 2 % 2, (accg, accu)[u % 2]
+            fwd_copy(u).wait()
+            t = slice_at(h, d)
+
+            def body(n, _, u=u, d=d, acc=acc, t=t):
+                cols = lanes(n * HN, HN)
+                acc[:, cols] += jnp.dot(
+                    X[0, t, :, part_lanes(d)], wbuf[pl.ds(u % 3 * W0, WIDE[d]), cols],
+                    preferred_element_type=F32,
+                )
+                return 0
+
+            lax.fori_loop(0, H // HN, body, 0)
+            if u + 3 < 4 * T:
+                fwd_copy(u + 3).start()
 
     def activate():
         def body(i, _):
@@ -287,7 +277,7 @@
             accu[rows, :] = silu
             return 0
 
-        lax.fori_loop(0, 2 * HR // 16, body, 0)
+        lax.fori_loop(0, G * R // 16, body, 0)
         for n in range(H // 128):
             act_t[n * 128:(n + 1) * 128, :] = act[:, n * 128:(n + 1) * 128].T
 
@@ -299,67 +289,70 @@
             dgu[rows, H:2 * H] = (grad * accu[rows, :]).astype(BF16)
             return 0
 
-        lax.fori_loop(0, 2 * HR // 16, body, 0)
+        lax.fori_loop(0, G * R // 16, body, 0)
 
     def part_copy(k, d):
         return pltpu.make_async_remote_copy(
-            src_ref=part.at[k, d, pl.ds(pl.multiple_of(other * R2, 16), R2), :],
-            dst_ref=part_in.at[k, d],
+            src_ref=part.at[k, pl.ds(pl.multiple_of(other * R, 16), R), part_lanes(d)],
+            dst_ref=part_in.at[k, :, part_lanes(d)],
             send_sem=part_s.at[k, d], recv_sem=part_r.at[k, d],
             device_id=pairdev, device_id_type=MESH,
         )
 
     def own_part(k, d):
-        return part.at[k, d, pl.ds(pl.multiple_of(g * R2, 16), R2), :]
+        return part.at[k, pl.ds(pl.multiple_of(g * R, 16), R), part_lanes(d)]
 
     def down(k):
         for d in range(2):
             t = snake((p + (1 + k if d else T - 1 - k)) % T, T)
-
-            def body(n, _, d=d, t=t):
-                part[k, d, :, lanes(n * WN, WN)] = jnp.dot(
-                    act[d * HR:(d + 1) * HR, :], wdv[:, lanes(t * W + n * WN, WN)],
+            WN = tile_of(WIDE[d], 256)
+
+            def body(n, _, d=d, t=t, WN=WN):
+                part[k, :, lanes(LOW[d] + n * WN, WN)] = jnp.dot(
+                    act[...], wdv[:, lanes(t * W + LOW[d] + n * WN, WN)],
                     preferred_element_type=F32,
                 ).astype(BF16)
                 return 0
 
-            lax.fori_loop(0, W // WN, body, 0)
+            lax.fori_loop(0, WIDE[d] // WN, body, 0)
             part_copy(k, d).start()
 
     def grad_act(h):
         pair_arrive(1, h)
+        for d in range(2):
+            t = slice_at(h, d)
+
+            def body(n, _, d=d, t=t):
+                ga[:, lanes(n * HN, HN)] += lax.dot_general(
+                    X[1, t, :, part_lanes(d)],
+                    wdv[pl.ds(pl.multiple_of(n * HN, 16), HN), lanes(t * W + LOW[d], WIDE[d])],
+                    (((1,), (1,)), ((), ())), preferred_element_type=F32,
+                )
+                return 0
+
+            lax.fori_loop(0, H // HN, body, 0)
+
+    FT = tile_of(H, 512)
+
+    def score_down(h, d):
+        t = slice_at(h, d)
+        WN = tile_of(WIDE[d], 256)
 
         def body(i, _):
-            d = i // (H // HN)
-            n = i % (H // HN)
-            off = d * h + (1 - d) * (T - h)
-            t = snake((p + off) % T, T)
-            ga[rows_of(d), lanes(n * HN, HN)] += lax.dot_general(
-                X[1, t, rows_of(d), :], wdv[pl.ds(pl.multiple_of(n * HN, 16), HN), lanes(t * W, W)],
-                (((1,), (1,)), ((), ())), preferred_element_type=F32,
-            )
-            return 0
-
-        lax.fori_loop(0, 2 * (H // HN), body, 0)
-
-    FT = tile_of(H, 512)
-
-    def score_down(t):
-        def body(i, _):
-            f = i // (W // WN)
-            n = i % (W // WN)
+            f = i // (WIDE[d] // WN)
+            n = i % (WIDE[d] // WN)
             fr = pl.ds(pl.multiple_of(f * FT, 16), FT)
             grad = jnp.dot(
-                act_t[fr, :], X[1, t, :, lanes(n * WN, WN)], preferred_element_type=F32
+                act_t[fr, :], X[1, t, :, lanes(LOW[d] + n * WN, WN)], preferred_element_type=F32
             )
-            value = jnp.abs(grad * wdv[fr, lanes(t * W + n * WN, WN)].astype(F32))
+            value = jnp.abs(grad * wdv[fr, lanes(t * W + LOW[d] + n * WN, WN)].astype(F32))
             total = imp_dn[fr, :]
             for q in range(WN // 128):
                 total += value[:, q * 128:(q + 1) * 128]
             imp_dn[fr, :] = total
             return 0
 
-        lax.fori_loop(0, (H // FT) * (W // WN), body, 0)
+        lax.fori_loop(0, (H // FT) * (WIDE[d] // WN), body, 0)
 
     NU = D // KB
 
@@ -382,7 +375,7 @@
                         xt[...], dgu[:, m * H + n * HN:m * H + (n + 1) * HN],
                         preferred_element_type=F32,
                     )
-                    value = jnp.abs(grad * wbuf[slot, m, :, n * HN:(n + 1) * HN].astype(F32))
+                    value = jnp.abs(grad * wbuf[pl.ds(pl.multiple_of((slot * 2 + m) * KB, KB), KB), n * HN:(n + 1) * HN].astype(F32))
                     imp_gu[:, n * HN:(n + 1) * HN] += jnp.sum(value.reshape(KB // 8, 8, HN), axis=0)
             return 0
 
@@ -390,13 +383,13 @@
 
     def sum_copy(k, d):
         return pltpu.make_async_remote_copy(
-            src_ref=own_part(k, d), dst_ref=sum_in.at[k, d],
+            src_ref=own_part(k, d), dst_ref=sum_in.at[k, :, part_lanes(d)],
             send_sem=sum_s.at[k, d], recv_sem=sum_r.at[k, d],
             device_id=ringdev(d), device_id_type=MESH,
         )
 
     def back_rows(k):
-        return part.at[T - 1, k % 2, pl.ds(pl.multiple_of(g * R2 + (k // 2) * C, 16), C), :]
+        return part.at[T - 1, pl.ds(pl.multiple_of(g * R + k * C, 16), C), :]
 
     def back_copy(k):
         return pltpu.make_async_remote_copy(
@@ -416,16 +409,16 @@
             if k > 0:
                 sum_copy(k - 1, d).wait_recv()
 
-            def body(i, _, d=d):
-                rows = pl.ds(pl.multiple_of(g * R2 + i * 16, 16), 16)
+            def body(i, _, cols=part_lanes(d)):
+                rows = pl.ds(pl.multiple_of(g * R + i * 16, 16), 16)
                 here = pl.ds(pl.multiple_of(i * 16, 16), 16)
-                total = part[k, d, rows, :].astype(F32) + part_in[k, d, here, :].astype(F32)
+                total = part[k, rows, cols].astype(F32) + part_in[k, here, cols].astype(F32)
                 if k > 0:
-                    total += sum_in[k - 1, d, here, :].astype(F32)
-                part[k, d, rows, :] = total.astype(BF16)
+                    total += sum_in[k - 1, here, cols].astype(F32)
+                part[k, rows, cols] = total.astype(BF16)
                 return 0
 
-            lax.fori_loop(0, R2 // 16, body, 0)
+            lax.fori_loop(0, R // 16, body, 0)
             if k < T - 1:
                 sum_copy(k, d).start()
         if k == T - 1:
@@ -463,8 +456,8 @@
             reduce_step(h - 2)
         arrive(1, h)
         grad_act(h - 1)
-        if h == 1:
-            score_down(tp)
+        for d in range(2):
+            score_down(h - 1, d)
     down(T - 1)
     grad_act(T - 1)
     gradients()
@@ -474,8 +467,8 @@
     score_gate_up(first, second)
     reduce_step(T - 1)
     score_gate_up(second, NU)
-    for h in range(1, T):
-        score_down(slice_at(h, 0))
+    for d in range(2):
+        score_down(T - 1, d)
     for n in range(H // 128):
         cols = slice(n * 128, (n + 1) * 128)
         value = jnp.sum(imp_gu[:, cols], axis=0, keepdims=True)
@@ -509,10 +502,10 @@
     G = lax.axis_size("grp")
     H = w_gate.shape[2]
     D = w_gate.shape[1]
-    NC = E // 2 if T <= 4 else 1
+    NC = E if T <= 4 else 1
     KB = tile_of(W, 512)
     rows = G * E * C
-    R2 = E // 2 * C
+    W0 = -(-W // 256) * 128
     dma = pltpu.SemaphoreType.DMA
     hbm = pl.BlockSpec(memory_space=pl.ANY)
     vmem = pl.BlockSpec(memory_space=pltpu.VMEM)
@@ -533,10 +526,10 @@
             pltpu.VMEM((H, rows), BF16),
             pltpu.VMEM((rows, 2 * H), BF16),
             pltpu.VMEM((H, D), BF16),
-            pltpu.VMEM((T, 2, G * R2, W), BF16),
-            pltpu.VMEM((T, 2, R2, W), BF16),
-            pltpu.VMEM((T - 1, 2, R2, W), BF16),
-            pltpu.VMEM((2, 2, KB, H), BF16),
+            pltpu.VMEM((T, rows, W), BF16),
+            pltpu.VMEM((T, E * C, W), BF16),
+            pltpu.VMEM((T - 1, E * C, W), BF16),
+            pltpu.VMEM((max(3 * W0, 4 * KB), H), BF16),
             pltpu.VMEM((KB, rows), BF16),
             pltpu.VMEM((8, H), F32),
             pltpu.VMEM((H, 128), F32),
@@ -549,7 +542,7 @@
             dma((T, 2)), dma((T, 2)),
             dma((T, 2)), dma((T, 2)),
             dma((E,)), dma((E,)),
-            dma((2, 2)), dma,
+            dma((3,)), dma((2, 2)), dma,
             dma((T,)), dma((T,)), dma((E * G,)), dma((E * G,)),
         ],
         compiler_params=pltpu.CompilerParams(

time: 192 us -> 190 us (0.990)
  the two profiles are of different devices: /device:TPU:26 before, /device:TPU:0 now
where the time goes in v3:
time: 190 us; the launch traced here: 187 us
  Pallas kernels  176 us (93%)
  local copies, waits for them, and re-layouts  5.84 us (3%)
  other arithmetic  5.31 us (3%)
    pallas_call x1, Pallas kernels, expert_call(): pl.pallas_call(functools.partial(expert_kernel, E, T, G, C, W, H, NC, KB)...  176 us

profile of v3, /device:TPU:0, one launch (start us, length us, event | category | flops | bytes accessed | tf_op | source)
XLA Modules:
  0.0 187.4 jit_solution(18430436810860028925)
XLA Ops:
  0.6 0.8 slice_bitcast_fusion.1
  1.4 0.8 slice_bitcast_fusion.3
  2.1 0.2 convert_reduce_fusion.1
  2.3 0.8 fusion.8
  3.1 0.8 multiply_add_fusion.1
  3.9 1.3 broadcast_in_dim.55.gain
  5.1 1.3 fusion.6.docs
  6.5 0.7 fusion.3.placing
  7.1 0.7 select_add_fusion.placed_gates
  7.8 0.1 fusion
  8.0 0.8 pad_maximum_fusion.picks
  8.8 175.6 %expert_layer.1 = (bf16[128,1536]{1,0:T(8,128)(2,1)}, f32[1,1024]{1,0:T(1,128)}) custom-call(bf16[128,1536]{1,0:T(8,128)(2,1)} %hidden.1, bf16[1,1536]{1,0:T(2,128)(2,1)} %broadcast_in_dim.55.gain, bf16[128,1536]{1,0:T(8,128)(2,1)} %upstream.1, bf16[320,128]{1,0:T(8,128)(2,1)} %fusion.3.placing, f32[320,128]{1,0:T(8,128)} %select_add_fusion.placed_gates, ...), custom_call_target="tpu_custom_call" | custom-call | flops 56371445760 | bytes 75497472 | tf_op jit(solution)/shard_map/expert_layer/pallas_call | solution.py:512
  184.4 1.8 copy.13
  186.2 1.3 copy.14

commit v4 on v3

--- a/solution.py
+++ b/solution.py
@@ -148,7 +148,6 @@
         )
 
     def send_blocks(a):
-        own_copy(a).start()
         for k in range(1, E):
             a2a_copy(a, k).start()
 
@@ -213,21 +212,19 @@
                 total += gate * jnp.dot(where, back[:, cols], preferred_element_type=F32)
             mixed[:, cols] = (hidden[:, cols].astype(F32) + total).astype(BF16)
 
-    def arrive(a, h):
-        for c in range(NC):
-            for d in range(2):
-                if h == 0:
-                    per = E // NC
-                    for k in range(c * per, (c + 1) * per) if d == 0 else ():
-                        if k == 0:
-                            own_copy(a).wait()
-                        else:
-                            a2a_copy(a, k).wait_recv()
+    def arrive(a, h, c):
+        if h == 0:
+            for k in range(c * (E // NC), (c + 1) * (E // NC)):
+                if k == 0:
+                    own_copy(a).wait()
                 else:
-                    ring_copy(a, h - 1, d, c, True).wait_recv()
-                if h < T - 1:
-                    ring_copy(a, h, d, c).start()
-                pair_copy(a, h, d, c).start()
+                    a2a_copy(a, k).wait_recv()
+        for d in range(2):
+            if h > 0:
+                ring_copy(a, h - 1, d, c, True).wait_recv()
+            if h < T - 1:
+                ring_copy(a, h, d, c).start()
+            pair_copy(a, h, d, c).start()
 
     def pair_arrive(a, h):
         for c in range(NC):
@@ -432,34 +429,49 @@
     imp_gu[...] = jnp.zeros(imp_gu.shape, F32)
     imp_dn[...] = jnp.zeros(imp_dn.shape, F32)
     place_rows()
+    own_copy(0).start()
     send_blocks(0)
     place_cot()
-
-    arrive(0, 0)
-    send_blocks(1)
+    own_copy(1).start()
+
+    rows_first = [(3 * c + h, 0, h, c) for c in range(NC) for h in range(T)]
+    rows_first += [(h + 1.5, 1, h, 0) for h in range(T)]
+    for _, a, h, c in sorted(rows_first):
+        if (a, h, c) == (0, T - 1, NC - 1):
+            forward(0)
+        arrive(a, h, c)
+        if (a, h, c) == (0, 0, NC - 1):
+            send_blocks(1)
+    later = [(h, c) for _, h, c in sorted((3 * c + h, h, c) for c in range(1, NC) for h in range(T))]
+
+    def arrive_next(n):
+        for h, c in later[:n]:
+            arrive(1, h, c)
+        del later[:n]
+
+    arrive_next(1)
     for h in range(1, T):
-        arrive(0, h)
-        forward(h - 1)
-        if h == min(2, T - 1):
-            arrive(1, 0)
-    forward(T - 1)
+        forward(h)
+        arrive_next(2)
     for c in grad_copies(0, 0):
         c.start()
     activate()
+    arrive_next(2)
     wd_copy().wait()
+    for k in range(T - 1):
+        down(k)
+        arrive_next(1)
+        if k == 1:
+            reduce_step(0)
+    arrive_next(len(later))
     for a in range(2):
         for k in range(1, E):
             a2a_copy(a, k).wait_send()
-    for h in range(1, T):
-        down(h - 1)
-        if h > 1:
-            reduce_step(h - 2)
-        arrive(1, h)
-        grad_act(h - 1)
-        for d in range(2):
-            score_down(h - 1, d)
     down(T - 1)
-    grad_act(T - 1)
+    for h in range(T):
+        grad_act(h)
+        if 0 < h < T - 2:
+            reduce_step(h)
     gradients()
     first, second = NU // 4, NU // 4 + NU // 3
     score_gate_up(0, first)
@@ -467,8 +479,9 @@
     score_gate_up(first, second)
     reduce_step(T - 1)
     score_gate_up(second, NU)
-    for d in range(2):
-        score_down(T - 1, d)
+    for h in range(T):
+        for d in range(2):
+            score_down(h, d)
     for n in range(H // 128):
         cols = slice(n * 128, (n + 1) * 128)
         value = jnp.sum(imp_gu[:, cols], axis=0, keepdims=True)

time: 190 us -> 193 us (1.016)
  Pallas kernels: 176 us -> 180 us
    pallas_call x1, Pallas kernels: 176 us -> 180 us  [expert_call(): pl.pallas_call(functools.partial(expert_kernel, E, T, G, C, W, H, NC, KB)...]
where the time goes in v4:
time: 193 us; the launch traced here: 192 us
  Pallas kernels  180 us (93%)
  local copies, waits for them, and re-layouts  5.84 us (3%)
  other arithmetic  5.31 us (3%)
    pallas_call x1, Pallas kernels, expert_call(): pl.pallas_call(functools.partial(expert_kernel, E, T, G, C, W, H, NC, KB)...  180 us

profile of v4, /device:TPU:0, one launch (start us, length us, event | category | flops | bytes accessed | tf_op | source)
XLA Modules:
  0.0 191.9 jit_solution(13994328485017763600)
XLA Ops:
  0.6 0.8 slice_bitcast_fusion.1
  1.4 0.8 slice_bitcast_fusion.3
  2.1 0.2 convert_reduce_fusion.1
  2.3 0.8 fusion.8
  3.1 0.8 multiply_add_fusion.1
  3.9 1.3 broadcast_in_dim.55.gain
  5.1 1.3 fusion.6.docs
  6.5 0.7 fusion.3.placing
  7.1 0.7 select_add_fusion.placed_gates
  7.8 0.1 fusion
  8.0 0.8 pad_maximum_fusion.picks
  8.8 180.1 %expert_layer.1 = (bf16[128,1536]{1,0:T(8,128)(2,1)}, f32[1,1024]{1,0:T(1,128)}) custom-call(bf16[128,1536]{1,0:T(8,128)(2,1)} %hidden.1, bf16[1,1536]{1,0:T(2,128)(2,1)} %broadcast_in_dim.55.gain, bf16[128,1536]{1,0:T(8,128)(2,1)} %upstream.1, bf16[320,128]{1,0:T(8,128)(2,1)} %fusion.3.placing, f32[320,128]{1,0:T(8,128)} %select_add_fusion.placed_gates, ...), custom_call_target="tpu_custom_call" | custom-call | flops 56371445760 | bytes 75497472 | tf_op jit(solution)/shard_map/expert_layer/pallas_call | solution.py:525
  188.8 1.8 copy.13
  190.6 1.3 copy.14
